TPU v7x, 256 devices: a whole 4x4x8 slice. The times are simulated.
256 devices in a mesh: grp: 8 (over x, y_hi), tp: 8 (over z), dp: 4 (over y_lo, core).
Axes of the slice: x: 4, y: 4 (y_hi: 2, y_lo: 2; y = y_hi * 2 + y_lo), z: 8, core: 2. Of those that a mesh axis runs over, the one named last changes fastest.
Arguments:
- prompt_hidden: bfloat16 [8192, 5120], P(('dp', 'grp'), 'tp'), parts along dimension 0, may hold values from -6 to 6
- w_kv: bfloat16 [5120, 2048], P('tp'), may hold values from -0.078125 to 0.078125
- resp_q: bfloat16 [32, 256, 8192], P(('dp', 'grp'), None, 'tp'), parts along dimension 0, may hold values from -28 to 28
- resp_kv: bfloat16 [32, 256, 2048], P(('dp', 'grp'), None, 'tp'), parts along dimension 0, may hold values from -28 to 28
- d_out: bfloat16 [32, 256, 8192], P(('dp', 'grp'), None, 'tp'), parts along dimension 0, may hold values from -96 to 96
- lengths: int32 [32], P(('dp', 'grp')), parts along dimension 0, may hold values from 32 to 256, as said below
Outputs:
- d_q: bfloat16 [32, 256, 8192], P(('dp', 'grp'), None, 'tp'), parts along dimension 0
- d_kv_resp: bfloat16 [32, 256, 2048], P(('dp', 'grp'), None, 'tp'), parts along dimension 0
- d_hidden: bfloat16 [8192, 5120], P(('dp', 'grp'), 'tp'), parts along dimension 0
- d_wkv: float32 [20480, 2048], P(('dp', 'tp'), 'grp'), parts along dimension 0
There are 4 independent parts, one for each index of `dp`. A program takes and returns all parts, laid end to end along the dimension named above; an argument that names none is the same for every part. Nothing has to cross between parts.
Inputs may be any that keep to these rules, and one draw needn't show every extreme that they name: `lengths`: the first response of every prompt has 256 live tokens.
All inputs are finite; a program needn't handle non-finite values.
Results may differ from a plain program's by a relative error of at most 0.035.
The roundings to bfloat16 on the way count: a program that leaves them out, or rounds other values in their place, can miss the bound.
Values may be sent and summed in bfloat16 or wider, within the bound.
A program may use at most 128 MiB of HBM per device.

v0:
```python
import jax
import jax.numpy as jnp
from jax import lax
from jax.sharding import PartitionSpec as P

HD = 128
GQ = 8
QB = 128


rope_theta = 1000000.0


def angles(positions):
    ladder = jnp.arange(HD // 2).astype(jnp.float32)
    frequency = rope_theta ** (-2.0 * ladder / HD)
    turned = positions.astype(jnp.float32)[:, None] * frequency[None, :]
    return (jnp.cos(turned), jnp.sin(turned))


def rotate(values, cosine, sine_part):
    half_width = values.shape[-1] // 2
    first_half = values[..., :half_width]
    second = values[..., half_width:]
    return jnp.concatenate(
        [first_half * cosine - second * sine_part, second * cosine + first_half * sine_part], -1
    )


def block_grads(q_block, key_rows, value_rows, grad_block, offset, prompt_len):
    score_scale = HD ** (-0.5)
    query_pos = offset + jnp.arange(q_block.shape[0])[:, None]
    key_pos = jnp.arange(key_rows.shape[0])[None, :]
    visible = (key_pos < prompt_len) | (key_pos - prompt_len <= query_pos)
    scores = (
        jnp.einsum("tgd,cd->gtc", q_block, key_rows, preferred_element_type=jnp.float32)
        * score_scale
    )
    scores = jnp.where(visible[None], scores, -jnp.inf)
    top_score = jnp.max(scores, -1, keepdims=True)
    raised = jnp.exp(scores - top_score)
    attend = raised / jnp.sum(raised, -1, keepdims=True)
    attend_b = attend.astype(jnp.bfloat16)
    output = jnp.einsum(
        "gtc,cd->gtd", attend_b, value_rows, preferred_element_type=jnp.float32
    ).astype(jnp.bfloat16)
    delta_row = jnp.sum(
        jnp.transpose(grad_block, (1, 0, 2)).astype(jnp.float32) * output.astype(jnp.float32), -1
    )
    d_attend = jnp.einsum("tgd,cd->gtc", grad_block, value_rows, preferred_element_type=jnp.float32)
    d_score = (attend * (d_attend - delta_row[..., None])).astype(jnp.bfloat16)
    d_query = (
        jnp.einsum("gtc,cd->gtd", d_score, key_rows, preferred_element_type=jnp.float32)
        * score_scale
    )
    d_key = (
        jnp.einsum("gtc,tgd->cd", d_score, q_block, preferred_element_type=jnp.float32)
        * score_scale
    )
    d_value = jnp.einsum("gtc,tgd->cd", attend_b, grad_block, preferred_element_type=jnp.float32)
    return (d_query, d_key, d_value)


def local(prompt_hidden, w_kv, resp_q, resp_kv, d_out, lengths):
    prompt_rows = prompt_hidden.shape[0]
    heads_here = resp_kv.shape[2] // (2 * HD)
    partial_kv = jnp.dot(prompt_hidden, w_kv, preferred_element_type=jnp.float32)
    my_heads = lax.psum_scatter(partial_kv, "tp", scatter_dimension=1, tiled=True).reshape(
        prompt_rows, heads_here, 2, HD
    )
    row_pos = lax.axis_index("grp") * prompt_rows + jnp.arange(prompt_rows, dtype=jnp.int32)
    cos_prompt, sin_prompt = angles(row_pos)
    prompt_keys = rotate(my_heads[:, :, 0], cos_prompt[:, None], sin_prompt[:, None])
    local_prefix = (
        jnp.stack([prompt_keys, my_heads[:, :, 1]], 2)
        .astype(jnp.bfloat16)
        .reshape(prompt_rows, heads_here * 2 * HD)
    )
    prefix = lax.all_gather(local_prefix, "grp", axis=0, tiled=True).reshape(-1, heads_here, 2, HD)
    prompt_len = prefix.shape[0]
    resp_count = resp_q.shape[0]
    resp_len = resp_q.shape[1]
    cos_resp, sin_resp = angles(prompt_len + jnp.arange(resp_len, dtype=jnp.int32))
    queries = rotate(
        resp_q.reshape(resp_count, resp_len, heads_here * GQ, HD).astype(jnp.float32),
        cos_resp[None, :, None],
        sin_resp[None, :, None],
    ).astype(jnp.bfloat16)
    own_pairs = resp_kv.reshape(resp_count, resp_len, heads_here, 2, HD)
    own_keys = rotate(
        own_pairs[:, :, :, 0].astype(jnp.float32), cos_resp[None, :, None], sin_resp[None, :, None]
    ).astype(jnp.bfloat16)
    own_values = own_pairs[:, :, :, 1]
    live_rows = jnp.arange(resp_len)[None, :] < lengths[:, None]
    masked = jnp.where(live_rows[:, :, None], d_out, jnp.zeros_like(d_out)).reshape(
        resp_count, resp_len, heads_here * GQ, HD
    )
    prefix_dk = jnp.zeros((prompt_len, HD), jnp.float32)
    prefix_dv = jnp.zeros((prompt_len, HD), jnp.float32)
    which_resp = 0
    block_dq = []
    own_dk = jnp.zeros((resp_len, HD), jnp.float32)
    own_dv = jnp.zeros((resp_len, HD), jnp.float32)
    for which_block in range(resp_len // QB):
        offset = which_block * QB
        reach_end = offset + QB
        q_block = queries[which_resp, offset:reach_end, 0:GQ]
        grad_block = masked[which_resp, offset:reach_end, 0:GQ]
        key_rows = jnp.concatenate([prefix[:, 0, 0], own_keys[which_resp, :reach_end, 0]], 0)
        value_rows = jnp.concatenate([prefix[:, 0, 1], own_values[which_resp, :reach_end, 0]], 0)

        def live_block(
            q_block=q_block,
            key_rows=key_rows,
            value_rows=value_rows,
            grad_block=grad_block,
            offset=offset,
        ):
            return block_grads(q_block, key_rows, value_rows, grad_block, offset, prompt_len)

        d_query, d_key, d_value = live_block()
        block_dq.append(d_query)
        prefix_dk = prefix_dk + d_key[:prompt_len]
        prefix_dv = prefix_dv + d_value[:prompt_len]
        own_dk = own_dk + jnp.pad(d_key[prompt_len:], ((0, resp_len - reach_end), (0, 0)))
        own_dv = own_dv + jnp.pad(d_value[prompt_len:], ((0, resp_len - reach_end), (0, 0)))
    query_row = [jnp.concatenate(block_dq, 1)]
    own_dk_row = [own_dk]
    own_dv_row = [own_dv]
    prefix_dk_heads = [prefix_dk]
    prefix_dv_heads = [prefix_dv]
    which_resp = 0
    stacked_q = jnp.stack([query_row[which_resp]], 0)
    stacked_q = stacked_q.reshape(heads_here * GQ, resp_len, HD).transpose(1, 0, 2)
    query_list = [stacked_q]
    stacked_dk = jnp.stack([own_dk_row[which_resp]], 0)
    stacked_dv = jnp.stack([own_dv_row[which_resp]], 0)
    turned_dk = rotate(stacked_dk, cos_resp[None], -sin_resp[None])
    pair_list = [
        jnp.stack([turned_dk, stacked_dv], 1)
        .transpose(2, 0, 1, 3)
        .reshape(resp_len, heads_here * 2 * HD)
    ]
    all_query = jnp.stack(query_list, 0)
    d_q = (
        rotate(all_query, cos_resp[None, :, None], -sin_resp[None, :, None])
        .astype(jnp.bfloat16)
        .reshape(resp_count, resp_len, heads_here * GQ * HD)
    )
    d_kv_resp = jnp.stack(pair_list, 0).astype(jnp.bfloat16)
    prefix_full = jnp.stack([jnp.stack(prefix_dk_heads, 0), jnp.stack(prefix_dv_heads, 0)], 1)
    prefix_full = prefix_full.transpose(2, 0, 1, 3).reshape(prompt_len, heads_here * 2 * HD)
    summed = lax.psum_scatter(prefix_full, "grp", scatter_dimension=0, tiled=True).reshape(
        prompt_rows, heads_here, 2, HD
    )
    grad_keys = rotate(summed[:, :, 0], cos_prompt[:, None], -sin_prompt[:, None])
    grad_rows = (
        jnp.stack([grad_keys, summed[:, :, 1]], 2)
        .astype(jnp.bfloat16)
        .reshape(prompt_rows, heads_here * 2 * HD)
    )
    grad_all = lax.all_gather(grad_rows, "tp", axis=1, tiled=True)
    d_hidden = lax.dot_general(
        grad_all, w_kv, (((1,), (1,)), ((), ())), preferred_element_type=jnp.float32
    ).astype(jnp.bfloat16)
    partial_w = lax.dot_general(
        prompt_hidden, grad_all, (((0,), (0,)), ((), ())), preferred_element_type=jnp.float32
    )
    d_wkv = lax.psum_scatter(partial_w, "grp", scatter_dimension=1, tiled=True)
    return (d_q, d_kv_resp, d_hidden, d_wkv)


def solution(mesh):
    return jax.shard_map(
        local,
        mesh=mesh,
        in_specs=(
            P(("dp", "grp"), "tp"),
            P("tp", None),
            P(("dp", "grp"), None, "tp"),
            P(("dp", "grp"), None, "tp"),
            P(("dp", "grp"), None, "tp"),
            P(("dp", "grp")),
        ),
        out_specs=(
            P(("dp", "grp"), None, "tp"),
            P(("dp", "grp"), None, "tp"),
            P(("dp", "grp"), "tp"),
            P(("dp", "tp"), "grp"),
        ),
        check_vma=False,
    )
```

profile of v0, /device:TPU:4, one launch (start us, length us, event | category | flops | bytes accessed | tf_op | source)
XLA Modules:
  0.0 392.8 jit_solution(3792139570380904023)
XLA Ops:
  7.2 1.7 copy-done
  8.9 3.3 fusion.106
  13.8 1.2 copy.108
  15.1 2.0 copy.113
  17.1 1.1 fusion.100
  18.2 2.4 copy.158
  20.6 2.4 copy.157
  25.4 1.2 fusion.44
  26.6 1.2 fusion.76
  27.8 1.1 broadcast_select_fusion
  29.8 2.8 subtract_convert_fusion.1
  32.6 24.7 %reduce-scatter.4.cloned.1.call-done = f32[256,256]{1,0:T(8,128)} async-done(((f32[256,2048]{1,0:T(8,128)}), f32[256,256]{1,0:T(8,128)}) %reduce-scatter.4.cloned.1.call-update) | async-done | bytes 262160 | tf_op jit(solution)/shard_map/reduce_scatter | solution.py:68
  57.3 1.8 copy.102
  60.9 1.0 fusion.69
  63.4 1.6 copy.160
  65.0 1.8 copy.161
  67.6 1.5 fusion.77
  69.1 1.2 fusion.33
  70.3 1.4 slice_bitcast_fusion.2
  71.7 3.0 fusion.28
  74.7 3.4 compare_or_fusion
  78.0 35.6 %all-gather.3.cloned.1.call-done = bf16[2048,256]{0,1:T(8,128)(2,1)} async-done(((bf16[256,256]{0,1:T(8,128)(2,1)}), bf16[2048,256]{0,1:T(8,128)(2,1)}) %all-gather.3.cloned.1.call-update) | async-done | bytes 1048592 | tf_op jit(solution)/shard_map/all_gather | solution.py:79
  113.6 2.3 fusion.98
  115.9 2.0 copy.159
  117.9 2.0 copy.155
  120.0 7.6 %fusion.103 = (f32[8,128]{1,0:T(8,128)S(1)}, f32[8,128,2176]{1,2,0:T(8,128)}) fusion(pred[128,2176]{0,1:T(8,128)(4,1)} %fusion.28, bf16[128,128]{1,0:T(8,128)(2,1)} %fusion.77, bf16[2048,128]{1,0:T(8,128)(2,1)} %bitcast.182, bf16[1,256,8,64]{3,1,2,0:T(8,128)(2,1)} %get-tuple-element.20, bf16[1,256,8,64]{3,1,2,0:T(8,128)(2,1)} %get-tuple-element.21), kind=kOutput, calls=%fused_computation.165 | convolution fusion | flops 580978816 | bytes 10276864 | tf_op jit(solution)/shard_map/sub | solution.py:41
  127.6 4.4 %fusion.17 = bf16[8,128,2176]{1,2,0:T(8,128)(2,1)S(1)} fusion(f32[8,128,2176]{1,2,0:T(8,128)} %get-tuple-element.46, f32[8,128]{1,0:T(8,128)S(1)} %get-tuple-element.45), kind=kLoop, calls=%fused_computation.29 | loop fusion | flops 4456448 | bytes 13373440 | tf_op jit(solution)/shard_map/convert_element_type | solution.py:43
  132.1 2.6 convolution_bitcast_fusion.1
  134.6 1.4 fusion.27
  136.1 2.4 fusion.5
  138.6 2.5 fusion.16
  141.1 7.7 %fusion.102 = (f32[8,128]{1,0:T(8,128)S(1)}, f32[8,128,2304]{1,2,0:T(8,128)}) fusion(pred[128,2304]{0,1:T(8,128)(4,1)} %compare_or_fusion, bf16[128,8,128]{2,0,1:T(8,128)(2,1)S(1)} %fusion.33, bf16[256,64]{1,0:T(8,128)(2,1)} %bitcast.196, bf16[256,64]{1,0:T(8,128)(2,1)} %bitcast.194, bf16[2048,128]{1,0:T(8,128)(2,1)} %bitcast.183), kind=kOutput, calls=%fused_computation.164 | convolution fusion | flops 615188736 | bytes 10588160 | tf_op jit(solution)/shard_map/sub | solution.py:41
  148.8 4.6 %fusion.14 = bf16[8,128,2304]{1,2,0:T(8,128)(2,1)S(1)} fusion(f32[8,128,2304]{1,2,0:T(8,128)} %get-tuple-element.44, f32[8,128]{1,0:T(8,128)S(1)} %get-tuple-element.43), kind=kLoop, calls=%fused_computation.22 | loop fusion | flops 4718592 | bytes 14159872 | tf_op jit(solution)/shard_map/convert_element_type | solution.py:43
  153.5 1.7 convolution_bitcast_fusion
  155.2 1.5 fusion.26
  156.7 2.4 fusion.3
  159.2 1.7 fusion.15
  162.8 1.5 pad_maximum_fusion
  164.4 79.4 %reduce-scatter.6.cloned.1.call-done = f32[256,256]{0,1:T(8,128)} async-done(((f32[2048,256]{0,1:T(8,128)}), f32[256,256]{0,1:T(8,128)}) %reduce-scatter.6.cloned.1.call-update) | async-done | bytes 262160 | tf_op jit(solution)/shard_map/reduce_scatter | solution.py:153
  247.0 38.9 %all-gather.5.cloned.1.call-done = bf16[256,2048]{0,1:T(8,128)(2,1)} async-done(((bf16[256,256]{0,1:T(8,128)(2,1)}), bf16[256,2048]{0,1:T(8,128)(2,1)}) %all-gather.5.cloned.1.call-update) | async-done | bytes 1048592 | tf_op jit(solution)/shard_map/all_gather | solution.py:162
  285.9 4.5 %convolution_bitcast_fusion.4 = f32[640,2048]{0,1:T(8,128)} fusion(bf16[256,2048]{0,1:T(8,128)(2,1)} %all-gather.5.cloned.1.call-done, bf16[256,640]{1,0:T(8,128)(2,1)S(1)} %copy-done.9), kind=kOutput, calls=%fused_computation.30 | convolution fusion | flops 671088640 | bytes 6619136 | tf_op jit(solution)/shard_map/dot_general | solution.py:166
  294.3 3.7 convolution_multiply_fusion
  298.0 4.0 %convolution_multiply_fusion.1 = f32[8,128,128]{2,1,0:T(8,128)S(1)} fusion(bf16[8,128,2304]{1,2,0:T(8,128)(2,1)} %copy-done.1, bf16[256,64]{1,0:T(8,128)(2,1)S(1)} %bitcast.197, bf16[256,64]{1,0:T(8,128)(2,1)S(1)} %bitcast.195, bf16[2048,128]{1,0:T(8,128)(2,1)} %bitcast.185), kind=kOutput, calls=%fused_computation.35 | convolution fusion | flops 605880320 | bytes 5832704 | tf_op jit(solution)/shard_map/gtc,cd->gtd/dot_general | solution.py:53
  302.8 1.0 copy.124
  303.8 2.0 copy.133
  305.9 3.0 convolution_convert_fusion
  308.9 75.2 %reduce-scatter.8.cloned.1.call-done = f32[640,256]{0,1:T(8,128)} async-done(((f32[640,2048]{0,1:T(8,128)}), f32[640,256]{0,1:T(8,128)}) %reduce-scatter.8.cloned.1.call-update) | async-done | bytes 655376 | tf_op jit(solution)/shard_map/reduce_scatter | solution.py:169
  384.1 2.2 copy.135
  (109 shorter events, 18.1 us)
Async XLA Ops:
  7.2 1.7 copy-start
  7.2 5.8 %copy-start.18 = (bf16[1,256,256]{2,1,0:T(8,128)(2,1)S(1)}, bf16[1,256,256]{2,1,0:T(8,128)(2,1)}, u32[]{:S(2)}) copy-start(bf16[1,256,256]{2,1,0:T(8,128)(2,1)} %param.9) | copy-start | bytes 393220
  7.2 50.1 %reduce-scatter.4.cloned.1.call-start = ((), (), s32[]{:S(2)}) async-start(), calls=%async_computation.3 | async-start | bytes 2359296 | tf_op jit(solution)/shard_map/reduce_scatter | solution.py:68
  12.3 101.4 %all-gather.3.cloned.1.call-start = ((), (), s32[]{:S(2)}) async-start(), calls=%async_computation.4 | async-start | bytes 1179648 | tf_op jit(solution)/shard_map/all_gather | solution.py:79
  23.0 5.9 %copy-start.21 = (f32[256]{0:T(256)}, f32[256]{0:T(256)S(1)}, u32[]{:S(2)}) copy-start(f32[256]{0:T(256)S(1)} %add_convert_fusion.2) | copy-start | bytes 3076
  62.6 181.1 %reduce-scatter.6.cloned.1.call-start = ((), (), s32[]{:S(2)}) async-start(), calls=%async_computation.5 | async-start | bytes 2359296 | tf_op jit(solution)/shard_map/reduce_scatter | solution.py:153
  127.6 8.5 %slice-start.4 = ((s8[8912896]{0:T(1024)(128)(4,1)}), s8[4194304]{0:T(1024)(128)(4,1)S(1)}, s32[]{:S(2)}) async-start(s8[8912896]{0:T(1024)(128)(4,1)} %bitcast.169), calls=%async_computation.12 | async-start | bytes 8388608
  127.6 8.5 %slice-start.5 = ((s8[8912896]{0:T(1024)(128)(4,1)}), s8[4194304]{0:T(1024)(128)(4,1)S(1)}, s32[]{:S(2)}) async-start(s8[8912896]{0:T(1024)(128)(4,1)} %bitcast.169), calls=%async_computation.13 | async-start | bytes 8388608
  132.0 2.6 copy-start.10
  132.0 2.6 copy-start.14
  132.0 2.6 copy-start.20
  132.0 4.0 %slice-start.6 = ((s8[8912896]{0:T(1024)(128)(4,1)}), s8[524288]{0:T(1024)(128)(4,1)S(1)}, s32[]{:S(2)}) async-start(s8[8912896]{0:T(1024)(128)(4,1)} %bitcast.169), calls=%async_computation.14 | async-start | bytes 1048576
  136.1 2.5 copy-start.6
  136.1 2.5 copy-start.7
  138.6 2.5 copy-start.2
  148.8 7.9 %slice-start = ((s8[9437184]{0:T(1024)(128)(4,1)}), s8[4194304]{0:T(1024)(128)(4,1)S(1)}, s32[]{:S(2)}) async-start(s8[9437184]{0:T(1024)(128)(4,1)} %bitcast.167), calls=%async_computation.8 | async-start | bytes 8388608
  148.8 7.9 %slice-start.1 = ((s8[9437184]{0:T(1024)(128)(4,1)}), s8[4194304]{0:T(1024)(128)(4,1)S(1)}, s32[]{:S(2)}) async-start(s8[9437184]{0:T(1024)(128)(4,1)} %bitcast.167), calls=%async_computation.9 | async-start | bytes 8388608
  153.4 1.7 copy-start.11
  153.5 1.7 copy-start.13
  153.5 1.7 copy-start.17
  153.5 3.2 slice-start.2
  155.1 5.7 %copy-start.5 = (f32[2304,128]{0,1:T(8,128)}, f32[2304,128]{0,1:T(8,128)S(1)}, u32[]{:S(2)}) copy-start(f32[2304,128]{0,1:T(8,128)S(1)} %convolution_bitcast_fusion) | copy-start | bytes 3538948
  159.2 2.4 copy-start.1
  159.2 2.4 copy-start.4
  159.2 3.2 copy-start.8
  162.4 1.9 copy-start.3
  162.8 82.9 %copy-start.23 = (f32[256]{0:T(256)S(1)}, f32[256]{0:T(256)}, u32[]{:S(2)}) copy-start(f32[256]{0:T(256)} %add_convert_fusion.3) | copy-start | bytes 3076
  162.8 123.1 %copy-start.9 = (bf16[256,640]{1,0:T(8,128)(2,1)S(1)}, bf16[256,640]{1,0:T(8,128)(2,1)}, u32[]{:S(2)}) copy-start(bf16[256,640]{1,0:T(8,128)(2,1)} %param.6) | copy-start | bytes 983044
  164.3 121.6 %all-gather.5.cloned.1.call-start = ((), (), s32[]{:S(2)}) async-start(), calls=%async_computation.6 | async-start | bytes 1179648 | tf_op jit(solution)/shard_map/all_gather | solution.py:162
  246.7 137.4 %reduce-scatter.8.cloned.1.call-start = ((), (), s32[]{:S(2)}) async-start(), calls=%async_computation.7 | async-start | bytes 5898240 | tf_op jit(solution)/shard_map/reduce_scatter | solution.py:169
  290.4 0.8 slice-start.3
  290.4 1.8 copy-start.22
  290.4 2.1 slice-start.7
  290.4 3.8 copy-start.19
  290.5 7.5 %copy-start.15 = (bf16[1,256,1,64]{3,1,2,0:T(8,128)(2,1)S(1)}, bf16[1,256,1,64]{3,1,2,0:T(8,128)(2,1)}, u32[]{:S(2)}) copy-start(bf16[1,256,1,64]{3,1,2,0:T(8,128)(2,1)} %get-tuple-element.36) | copy-start | bytes 98308
  290.5 7.5 %copy-start.16 = (bf16[1,256,1,64]{3,1,2,0:T(8,128)(2,1)S(1)}, bf16[1,256,1,64]{3,1,2,0:T(8,128)(2,1)}, u32[]{:S(2)}) copy-start(bf16[1,256,1,64]{3,1,2,0:T(8,128)(2,1)} %get-tuple-element.37) | copy-start | bytes 98308
  298.0 4.0 %copy-start.12 = (f32[256,64]{1,0:T(8,128)S(1)}, f32[256,64]{1,0:T(8,128)}, u32[]{:S(2)}) copy-start(f32[256,64]{1,0:T(8,128)} %get-tuple-element.40) | copy-start | bytes 196612
Sparse Core Ops, SparseCore 0:
  12.4 44.8 reduce-scatter.3
  62.8 50.8 all-gather.2
  164.4 79.2 reduce-scatter.5
  246.8 39.0 all-gather.4
  290.6 93.4 reduce-scatter.7
where the time goes:
time: 396 us; the launch traced here: 393 us
  waiting for transfers between devices  254 us (64%)
  matrix products  50 us (13%)
  local copies, waits for them, and re-layouts  38.3 us (10%)
  other arithmetic  34.8 us (9%)
  between operations  15 us (4%)
    reduce_scatter x1, waiting for transfers between devices, local(): lax.psum_scatter(prefix_full, 'grp', scatter_dimension=0, tiled=True)  79.4 us
    reduce_scatter x1, waiting for transfers between devices, local(): d_wkv = lax.psum_scatter(partial_w, 'grp', scatter_dimension=1, tiled=True)  75.2 us
    all_gather x1, waiting for transfers between devices, local(): grad_all = lax.all_gather(grad_rows, 'tp', axis=1, tiled=True)  38.9 us
    all_gather x1, waiting for transfers between devices, local(): lax.all_gather(local_prefix, 'grp', axis=0, tiled=True)  35.6 us
    unnamed x74, local copies, waits for them, and re-layouts  24.9 us
    reduce_scatter x1, waiting for transfers between devices, local(): lax.psum_scatter(partial_kv, 'tp', scatter_dimension=1, tiled=True)  24.7 us
    sub x2, matrix products, block_grads(): raised = jnp.exp(scores - top_score)  15.3 us
    convert_element_type x2, other arithmetic, block_grads(): attend_b = attend.astype(jnp.bfloat16)  9.03 us
  transfers between devices with their start and end apart: 5, of which 5 were waited for; matrix products, arithmetic and copies ran while one was open for 13% of the time, Pallas kernels for 0%

commit v1 on v0

v1 whole, which is shorter than its diff:
```python
import functools

import jax
import jax.numpy as jnp
import numpy as np
from jax import lax
from jax.experimental import pallas as pl
from jax.experimental.pallas import tpu as pltpu
from jax.sharding import PartitionSpec as P

HD = 128
GQ = 8
THETA = 1000000.0
SCALE = HD**-0.5
MESH = pl.DeviceIdType.MESH
BF = jnp.bfloat16
F32 = jnp.float32


def tables(rows, groups):
    ladder = np.arange(HD // 2)
    frequency = (THETA ** (-2.0 * ladder / HD)).astype(np.float32).astype(np.float64)

    def both(positions):
        turned = positions[:, None] * frequency[None, :]
        cos, sin = np.cos(turned), np.sin(turned)
        return np.concatenate([cos, cos, -sin, sin], 1).astype(np.float32)

    return both(np.arange(rows)), both(np.arange(groups) * rows)


def dot(a, b):
    return lax.dot_general(a, b, (((1,), (0,)), ((), ())), preferred_element_type=F32)


def rotate(v, cos, sin):
    return v * cos + pltpu.roll(v, HD // 2, 1) * sin


def turned_tables(base_ref, start_ref, block):
    cos, sin = base_ref[:, :HD], base_ref[:, HD:]
    turn = start_ref[block]
    cos0, sin0 = turn[:, :HD], turn[:, HD:]
    return cos * cos0 - sin * sin0, sin * cos0 + cos * sin0


def kernel(
    nx, nt, x_ref, w_ref, q_ref, do_ref, kv_ref, len_ref, base_ref, start_ref,
    dq_ref, dkv_ref, dh_ref, dw_ref,
    q_rows, q_cols, g_rows, g_cols, kv, kv_t, e, top, low, delta, dq_t, cos_r, sin_r,
    b_send, b_recv, raw, x_t, grad_send, grad_recv, heads, cols, dh_acc,
    b_ss, b_rs, x_ss, x_rs, c_ss, c_rs, e_ss, e_rs, f_ss, f_rs, a_ss, a_rs,
):
    T = x_ref.shape[0]
    D = x_ref.shape[1]
    H = T // 2
    W2 = 2 * HD
    NG = 2 * nx
    half = nt // 2
    own = NG
    grp, tp, dp = lax.axis_index("grp"), lax.axis_index("tp"), lax.axis_index("dp")
    x, y = grp // 2, grp % 2

    def offset(k):
        j = k % 4
        return j + j // 2 - 2 * (j // 3), k // 4

    def peer(k):
        dx, dy = offset(k)
        return ((x + dx) % nx) * 2 + (y + dy) % 2

    def source(k):
        dx, dy = offset(k)
        return ((x - dx + nx) % nx) * 2 + (y + dy) % 2

    def on_grp(other):
        return (other, tp, dp)

    ring = [(grp, (tp + 1) % nt, dp), (grp, (tp + nt - 1) % nt, dp)]

    def remote(src, dst, ss, rs, device):
        return pltpu.make_async_remote_copy(
            src_ref=src, dst_ref=dst, send_sem=ss, recv_sem=rs, device_id=device, device_id_type=MESH
        )

    started = []

    def go(copy):
        copy.start()
        started.append(copy)

    barrier = pltpu.get_barrier_semaphore()
    for k in range(1, NG):
        pl.semaphore_signal(barrier, inc=1, device_id=on_grp(peer(k)), device_id_type=MESH)
    for device in ring:
        pl.semaphore_signal(barrier, inc=1, device_id=device, device_id_type=MESH)

    def part(h):
        at = pl.ds(pl.multiple_of(h * W2, W2), W2)
        return dot(x_ref[...], w_ref[:, at])

    def rows(d, c):
        return slice(0, H) if (d + c) % 2 == 0 else slice(H, T)

    def b_copy(d, s, c):
        return remote(b_send.at[d, s, c], b_recv.at[d, s, c], b_ss.at[d, s, c], b_rs.at[d, s, c], ring[d])

    def x_copy(src, dst, i, to):
        return remote(x_t.at[src], x_t.at[dst], x_ss.at[dst, i], x_rs.at[dst, i], on_grp(peer(to)))

    def x_half(src, dst, i, to):
        at = pl.ds(i * (D // 2), D // 2)
        return remote(
            x_t.at[src, at], x_t.at[dst, at], x_ss.at[dst, i], x_rs.at[dst, i], on_grp(peer(to))
        )

    far = part((tp + half) % nt)
    for d in range(2):
        b_send[d, 0, 0] = far[rows(d, 0)].astype(BF)
    x_t[0] = x_ref[...].astype(F32).T.astype(BF)
    pl.semaphore_wait(barrier, NG - 1 + 2)
    for d in range(2):
        go(b_copy(d, 0, 0))

    def prep_tables():
        c, s = turned_tables(base_ref, start_ref, NG)
        cos_r[...] = c
        sin_r[...] = s
        dq_t[...] = jnp.zeros_like(dq_t)

    def prep(c):
        def run():
            at = slice(c * HD, (c + 1) * HD)
            ct = slice(c * T, (c + 1) * T)
            live = lax.broadcasted_iota(jnp.int32, (T, HD), 0) < len_ref[0]
            qf = rotate(q_ref[:, at].astype(F32), cos_r[...], sin_r[...])
            q_rows[c] = qf.astype(BF)
            q_cols[:, ct] = qf.T.astype(BF)
            gf = jnp.where(live, do_ref[:, at].astype(F32), 0.0)
            g_rows[c] = gf.astype(BF)
            g_cols[:, ct] = gf.T.astype(BF)

        return run

    def prep_own():
        kv[own, :, :HD] = rotate(kv_ref[:, :HD].astype(F32), cos_r[...], sin_r[...]).astype(BF)
        kv[own, :, HD:] = kv_ref[:, HD:]

    def scores(p, is_own):
        kv_t[p] = kv[p].astype(F32).T.astype(BF)
        k = kv[p, :, :HD]
        if is_own:
            visible = lax.broadcasted_iota(jnp.int32, (T, T), 0) <= lax.broadcasted_iota(
                jnp.int32, (T, T), 1
            )
        for c in range(GQ):
            ct = slice(c * T, (c + 1) * T)
            s = dot(k, q_cols[:, ct]) * SCALE
            if is_own:
                s = jnp.where(visible, s, -jnp.inf)
            m = jnp.max(s, axis=0, keepdims=True)
            raised = jnp.exp(s - m)
            e[p, :, ct] = raised
            top[p, :, ct] = m
            low[p, :, ct] = jnp.sum(raised, axis=0, keepdims=True)

    fillers = [prep_tables] + [prep(c) for c in range(GQ)] + [prep_own]

    def fill(count):
        for _ in range(count):
            if fillers:
                fillers.pop(0)()

    for s in range(1, half):
        for d in range(2):
            sign = 1 if d == 0 else nt - 1
            raw[d] = part((tp + sign * (half - s)) % nt)
        for c in (1, 0):
            for d in range(2):
                v = raw[d, rows(d, c)]
                if c == 0 or s > 1:
                    b_copy(d, s - 1, c).wait_recv()
                    v = v + b_recv[d, s - 1, c].astype(F32)
                b_send[d, s, c] = v.astype(BF)
                go(b_copy(d, s, c))
            if s == 1 and c == 1:
                for k in (1, 2, 4):
                    go(x_copy(0, k, 0, k))
            fill(2)
    fill(len(fillers))
    raw[0] = part(tp)
    scores(own, True)
    for c in (1, 0):
        for d in range(2):
            if c == 0 or half > 1:
                b_copy(d, half - 1, c).wait_recv()
                raw[0, rows(d, c)] = raw[0, rows(d, c)] + b_recv[d, half - 1, c].astype(F32)
    cos_p, sin_p = turned_tables(base_ref, start_ref, grp)
    kv[0, :, :HD] = rotate(raw[0, :, :HD], cos_p, sin_p).astype(BF)
    kv[0, :, HD:] = raw[0, :, HD:].astype(BF)

    def c_copy(k):
        return remote(kv.at[0], kv.at[k], c_ss.at[k], c_rs.at[k], on_grp(peer(k)))

    for k in range(1, NG):
        go(c_copy(k))
    scores(0, False)

    def score_step(k, carry):
        c_copy(k).wait_recv()
        scores(k, False)
        return carry

    lax.fori_loop(1, NG, score_step, 0)
    for k in (1, 2, 4):
        x_copy(0, k, 0, k).wait_recv()
    go(x_half(1, 3, 0, 1))
    go(x_half(2, 3, 1, 2))
    go(x_copy(4, 5, 0, 1))
    go(x_copy(4, 6, 0, 2))

    m = functools.reduce(jnp.maximum, [top[p] for p in range(NG + 1)])
    weights = [jnp.exp(top[p] - m) for p in range(NG + 1)]
    total = functools.reduce(jnp.add, [weights[p] * low[p] for p in range(NG + 1)])
    inverse = 1.0 / total
    for p in range(NG + 1):
        top[p] = weights[p] * inverse
    for c in range(GQ):
        ct = slice(c * T, (c + 1) * T)
        acc = jnp.zeros((HD, T), F32)
        for p in range(NG + 1):
            acc = acc + dot(kv_t[p, HD:], (e[p, :, ct] * top[p, :, ct]).astype(BF))
        delta[:, ct] = jnp.sum(
            acc.astype(BF).astype(F32) * g_cols[:, ct].astype(F32), axis=0, keepdims=True
        )

    def backward(p):
        v = kv[p, :, HD:]
        dk = jnp.zeros((T, HD), F32)
        dv = jnp.zeros((T, HD), F32)
        for c in range(GQ):
            ct = slice(c * T, (c + 1) * T)
            a = e[p, :, ct] * top[p, :, ct]
            da = dot(v, g_cols[:, ct])
            ds = (a * (da - delta[:, ct])).astype(BF)
            dv = dv + dot(a.astype(BF), g_rows[c])
            dk = dk + dot(ds, q_rows[c])
            dq_t[:, ct] += dot(kv_t[p, :HD], ds)
        return dk * SCALE, dv

    def e_copy(k):
        return remote(
            grad_send.at[k], grad_recv.at[k], e_ss.at[k], e_rs.at[k], on_grp(source(k))
        )

    def grad_step(i, carry):
        k = NG - 1 - i
        dk, dv = backward(k)
        grad_send[k, :, :HD] = dk.astype(BF)
        grad_send[k, :, HD:] = dv.astype(BF)
        e_copy(k).start()
        return carry

    lax.fori_loop(0, 3, grad_step, 0)
    for k in (5, 6):
        x_copy(4, k, 0, 1).wait_recv()
    go(x_half(5, 7, 0, 1))
    go(x_half(6, 7, 1, 2))
    lax.fori_loop(3, NG - 1, grad_step, 0)
    dk, dv = backward(own)
    dkv_ref[:, :HD] = rotate(dk, cos_r[...], -sin_r[...]).astype(BF)
    dkv_ref[:, HD:] = dv.astype(BF)
    dk, dv = backward(0)
    raw[0, :, :HD] = dk
    raw[0, :, HD:] = dv

    def sum_step(i, carry):
        k = NG - 1 - i
        e_copy(k).wait_recv()
        raw[0] = raw[0] + grad_recv[k].astype(F32)
        return carry

    lax.fori_loop(0, NG - 1, sum_step, 0)
    cos_p, sin_p = turned_tables(base_ref, start_ref, grp)
    heads[0, :, :HD] = rotate(raw[0, :, :HD], cos_p, -sin_p).astype(BF)
    heads[0, :, HD:] = raw[0, :, HD:].astype(BF)

    def f_copy(d, s, c):
        src, dst = ((nt - s) % nt, nt - s - 1) if d == 0 else (s, s + 1)
        at = pl.ds(c * H, H)
        return remote(
            heads.at[src, at], heads.at[dst, at], f_ss.at[d, s, c], f_rs.at[d, s, c], ring[d]
        )

    def a_copy(slot):
        return remote(
            heads.at[slot], cols.at[grp], a_ss.at[slot], a_rs.at[grp], on_grp((tp + slot) % nt)
        )

    def pass_on(slot):
        @pl.when((tp + slot) % nt != grp)
        def _():
            a_copy(slot).start()

    def hidden(slot, first):
        h = (tp + slot) % nt
        at = pl.ds(pl.multiple_of(h * W2, W2), W2)
        term = lax.dot_general(
            heads[slot], w_ref[:, at], (((1,), (1,)), ((), ())), preferred_element_type=F32
        )
        if first:
            dh_acc[...] = term
        else:
            dh_acc[...] += term

    def query_out(c):
        ct = slice(c * T, (c + 1) * T)
        v = dq_t[:, ct].T * SCALE
        dq_ref[:, c * HD : (c + 1) * HD] = rotate(v, cos_r[...], -sin_r[...]).astype(BF)

    for c in range(2):
        for d in range(2):
            if half > 1 or c == d:
                go(f_copy(d, 0, c))
    pass_on(0)
    hidden(0, True)
    for c in range(4):
        query_out(c)
    for s in range(1, half):
        for c in range(2):
            for d in range(2):
                f_copy(d, s - 1, c).wait_recv()
                if s < half - 1 or c == d:
                    go(f_copy(d, s, c))
        for slot in (nt - s, s):
            pass_on(slot)
            hidden(slot, False)
        if s == 1:
            for c in range(4, GQ):
                query_out(c)
    f_copy(0, half - 1, 0).wait_recv()
    f_copy(1, half - 1, 1).wait_recv()
    pass_on(half)
    hidden(half, False)
    dh_ref[...] = dh_acc[...].astype(BF)

    for i in range(2):
        x_half(1, 3, i, 1).wait_recv()
        x_half(1, 7, i, 1).wait_recv()
    dw_ref[...] = dot(x_t[0], heads[(grp - tp + nt) % nt])

    def weight_step(k, carry):
        other = source(k)
        remote(
            heads.at[0], cols.at[other], a_ss.at[0], a_rs.at[other], on_grp(peer(1))
        ).wait_recv()
        dw_ref[...] += dot(x_t[k], cols[other])
        return carry

    lax.fori_loop(1, NG, weight_step, 0)

    for copy in started:
        copy.wait_send()

    def end_step(k, carry):
        e_copy(k).wait_send()
        return carry

    lax.fori_loop(1, NG, end_step, 0)
    for slot in range(nt):

        @pl.when((tp + slot) % nt != grp)
        def _():
            a_copy(slot).wait_send()


def local(nx, nt, prompt_hidden, w_kv, resp_q, resp_kv, d_out, lengths):
    T, D = prompt_hidden.shape
    NG = 2 * nx
    W2 = 2 * HD
    base, start = tables(T, NG + 1)
    start = start[:, None]
    vm = pl.BlockSpec(memory_space=pltpu.VMEM)
    dma = pltpu.SemaphoreType.DMA
    half = nt // 2
    dq, dkv, dh, dw = pl.pallas_call(
        functools.partial(kernel, nx, nt),
        out_shape=(
            jax.ShapeDtypeStruct((T, GQ * HD), BF),
            jax.ShapeDtypeStruct((T, W2), BF),
            jax.ShapeDtypeStruct((T, D), BF),
            jax.ShapeDtypeStruct((D, W2), F32),
        ),
        in_specs=[vm] * 5 + [pl.BlockSpec(memory_space=pltpu.SMEM)] + [vm] * 2,
        out_specs=(vm,) * 4,
        scratch_shapes=[
            pltpu.VMEM((GQ, T, HD), BF),
            pltpu.VMEM((HD, GQ * T), BF),
            pltpu.VMEM((GQ, T, HD), BF),
            pltpu.VMEM((HD, GQ * T), BF),
            pltpu.VMEM((NG + 1, T, W2), BF),
            pltpu.VMEM((NG + 1, W2, T), BF),
            pltpu.VMEM((NG + 1, T, GQ * T), F32),
            pltpu.VMEM((NG + 1, 1, GQ * T), F32),
            pltpu.VMEM((NG + 1, 1, GQ * T), F32),
            pltpu.VMEM((1, GQ * T), F32),
            pltpu.VMEM((HD, GQ * T), F32),
            pltpu.VMEM((T, HD), F32),
            pltpu.VMEM((T, HD), F32),
            pltpu.VMEM((2, half, 2, T // 2, W2), BF),
            pltpu.VMEM((2, half, 2, T // 2, W2), BF),
            pltpu.VMEM((2, T, W2), F32),
            pltpu.VMEM((NG, D, T), BF),
            pltpu.VMEM((NG, T, W2), BF),
            pltpu.VMEM((NG, T, W2), BF),
            pltpu.VMEM((nt, T, W2), BF),
            pltpu.VMEM((NG, T, W2), BF),
            pltpu.VMEM((T, D), F32),
            dma((2, half, 2)),
            dma((2, half, 2)),
            dma((NG, 2)),
            dma((NG, 2)),
            dma((NG,)),
            dma((NG,)),
            dma((NG,)),
            dma((NG,)),
            dma((2, half, 2)),
            dma((2, half, 2)),
            dma((nt,)),
            dma((NG,)),
        ],
        compiler_params=pltpu.CompilerParams(
            collective_id=0, has_side_effects=True, vmem_limit_bytes=60 * 2**20
        ),
        name="prefix_attention_backward",
    )(
        prompt_hidden,
        w_kv,
        resp_q.reshape(T, GQ * HD),
        d_out.reshape(T, GQ * HD),
        resp_kv.reshape(T, W2),
        lengths,
        jnp.asarray(base),
        jnp.asarray(start),
    )
    return dq[None], dkv[None], dh, dw


def solution(mesh):
    nx = mesh.shape["grp"] // 2
    nt = mesh.shape["tp"]
    return jax.shard_map(
        functools.partial(local, nx, nt),
        mesh=mesh,
        in_specs=(
            P(("dp", "grp"), "tp"),
            P("tp", None),
            P(("dp", "grp"), None, "tp"),
            P(("dp", "grp"), None, "tp"),
            P(("dp", "grp"), None, "tp"),
            P(("dp", "grp")),
        ),
        out_specs=(
            P(("dp", "grp"), None, "tp"),
            P(("dp", "grp"), None, "tp"),
            P(("dp", "grp"), "tp"),
            P(("dp", "tp"), "grp"),
        ),
        check_vma=False,
    )
```

time: 396 us -> 105 us (0.27)
  waiting for transfers between devices: 254 us -> 0 us
  Pallas kernels: 0 us -> 95.6 us
  matrix products: 50 us -> 0 us
  other arithmetic: 34.8 us -> 0 us
  local copies, waits for them, and re-layouts: 38.3 us -> 7.12 us
  between operations: 15 us -> 1.29 us
    reduce_scatter x3 -> x0, waiting for transfers between devices: 179 us -> none  [the longest x1 79.4 us: local(): lax.psum_scatter(prefix_full, 'grp', scatter_dimension=0, tiled=True)]
    pallas_call x0 -> x1, Pallas kernels: none -> 95.6 us  [local(): pl.pallas_call(functools.partial(kernel, nx, nt), out_shape=(jax.ShapeDty...]
    all_gather x2 -> x0, waiting for transfers between devices: 74.5 us -> none  [the longest x1 38.9 us: local(): grad_all = lax.all_gather(grad_rows, 'tp', axis=1, tiled=True)]
    dot_general x13 -> x0, matrix products: 34.7 us -> none  [the longest x2 7.69 us: block_grads(): jnp.einsum('gtc,cd->gtd', d_score, key_rows, preferred_element_type=jnp.f...]
    unnamed x74 -> x4, local copies, waits for them, and re-layouts: 24.9 us -> 7.12 us
    sub x2 -> x0, matrix products: 15.3 us -> none  [block_grads(): raised = jnp.exp(scores - top_score)]
    another operation x17 -> x0, other arithmetic: 11.3 us -> none
    convert_element_type x5 -> x0, other arithmetic: 9.64 us -> none  [the longest x2 9.03 us: block_grads(): attend_b = attend.astype(jnp.bfloat16)]
  transfers between devices with their start and end apart: 5 -> 0, of which waited for: 5 -> 0; matrix products, arithmetic and copies ran while one was open for 13% -> 0% of each run, Pallas kernels for 0% -> 0%
where the time goes in v1:
time: 105 us; the launch traced here: 104 us
  Pallas kernels  95.6 us (91%)
  local copies, waits for them, and re-layouts  7.12 us (7%)
  between operations  1.29 us (1%)
    pallas_call x1, Pallas kernels, local(): pl.pallas_call(functools.partial(kernel, nx, nt), out_shape=(jax.ShapeDty...  95.6 us
    unnamed x4, local copies, waits for them, and re-layouts  7.12 us

profile of v1, /device:TPU:4, one launch (start us, length us, event | category | flops | bytes accessed | tf_op | source)
XLA Modules:
  0.0 104.0 jit_solution(2029405444828473271)
XLA Ops:
  1.3 95.6 %prefix_attention_backward.1 = (bf16[256,1024]{1,0:T(8,128)(2,1)}, bf16[256,256]{1,0:T(8,128)(2,1)}, bf16[256,640]{1,0:T(8,128)(2,1)}, f32[640,256]{1,0:T(8,128)}) custom-call(bf16[256,640]{1,0:T(8,128)(2,1)} %x_ref.1, bf16[640,2048]{1,0:T(8,128)(2,1)} %w_ref.1, bf16[256,1024]{1,0:T(8,128)(2,1)} %bitcast.5, bf16[256,1024]{1,0:T(8,128)(2,1)} %bitcast.6, ...), custom_call_target="tpu_custom_call" | custom-call | tf_op jit(solution)/shard_map/prefix_attention_backward/pallas_call | solution.py:386
  96.9 1.9 %copy.17 = bf16[1,256,1024]{2,1,0:T(8,128)(2,1)} copy(bf16[1,256,1024]{2,1,0:T(8,128)(2,1)} %bitcast.7) | data formatting | bytes 1048576
  98.7 1.6 %copy.18 = bf16[1,256,256]{2,1,0:T(8,128)(2,1)} copy(bf16[1,256,256]{2,1,0:T(8,128)(2,1)} %bitcast.9) | data formatting | bytes 262144
  100.3 1.7 %copy.19 = bf16[256,640]{1,0:T(8,128)(2,1)} copy(bf16[256,640]{1,0:T(8,128)(2,1)} %get-tuple-element.18) | data formatting | bytes 655360
  102.0 2.0 %copy.20 = f32[640,256]{1,0:T(8,128)} copy(f32[640,256]{1,0:T(8,128)} %get-tuple-element.19) | data formatting | bytes 1310720

commit v2 on v1

v2 whole, which is shorter than its diff:
```python
import functools

import jax
import jax.numpy as jnp
import numpy as np
from jax import lax
from jax.experimental import pallas as pl
from jax.experimental.pallas import tpu as pltpu
from jax.sharding import PartitionSpec as P

HD = 128
GQ = 8
THETA = 1000000.0
SCALE = HD**-0.5
MESH = pl.DeviceIdType.MESH
BF = jnp.bfloat16
F32 = jnp.float32


def tables(rows, groups):
    ladder = np.arange(HD // 2)
    frequency = (THETA ** (-2.0 * ladder / HD)).astype(np.float32).astype(np.float64)

    def both(positions):
        turned = positions[:, None] * frequency[None, :]
        cos, sin = np.cos(turned), np.sin(turned)
        return np.concatenate([cos, cos, -sin, sin], 1).astype(np.float32)

    return both(np.arange(rows)), both(np.arange(groups) * rows)


def dot(a, b):
    return lax.dot_general(a, b, (((1,), (0,)), ((), ())), preferred_element_type=F32)


def rotate(v, cos, sin):
    return v * cos + pltpu.roll(v, HD // 2, 1) * sin


def turned_tables(base_ref, start_ref, block):
    cos, sin = base_ref[:, :HD], base_ref[:, HD:]
    turn = start_ref[block]
    cos0, sin0 = turn[:, :HD], turn[:, HD:]
    return cos * cos0 - sin * sin0, sin * cos0 + cos * sin0


def kernel(
    nx, nt, x_ref, w_ref, q_ref, do_ref, kv_ref, len_ref, base_ref, start_ref,
    dq_ref, dkv_ref, dh_ref, dw_ref,
    q_rows, q_cols, g_rows, g_cols, kb, vb, kt, vt, e, top, low, delta, ds_all, o_t, cos_r, sin_r,
    b_send, b_recv, raw, mine, x_t, grad_send, grad_recv, heads, cols, dh_acc,
    b_ss, b_rs, x_ss, x_rs, c_ss, c_rs, e_ss, e_rs, f_ss, f_rs, a_ss, a_rs,
):
    T = x_ref.shape[0]
    D = x_ref.shape[1]
    H = T // 2
    W2 = 2 * HD
    NG = 2 * nx
    own = NG
    kv = (kb, vb)
    grp, tp, dp = lax.axis_index("grp"), lax.axis_index("tp"), lax.axis_index("dp")
    x, y = grp // 2, grp % 2

    def offset(k):
        j = k % 4
        return j + j // 2 - 2 * (j // 3), k // 4

    def peer(k):
        dx, dy = offset(k)
        return ((x + dx) % nx) * 2 + (y + dy) % 2

    def source(k):
        dx, dy = offset(k)
        return ((x - dx + nx) % nx) * 2 + (y + dy) % 2

    def on_grp(other):
        return (other, tp, dp)

    def on_tp(step):
        return (grp, (tp + step + nt) % nt, dp)

    def remote(src, dst, ss, rs, device):
        return pltpu.make_async_remote_copy(
            src_ref=src, dst_ref=dst, send_sem=ss, recv_sem=rs, device_id=device, device_id_type=MESH
        )

    started = []

    def go(copy):
        copy.start()
        started.append(copy)

    barrier = pltpu.get_barrier_semaphore()
    for k in range(1, NG):
        pl.semaphore_signal(barrier, inc=1, device_id=on_grp(peer(k)), device_id_type=MESH)
    for step in range(1, nt):
        pl.semaphore_signal(barrier, inc=1, device_id=on_tp(step), device_id_type=MESH)

    def part(h, u):
        at = pl.ds(pl.multiple_of(h * W2 + u * HD, HD), HD)
        return dot(x_ref[...], w_ref[:, at])

    def b_copy(u, d, i):
        step = (2, 1, 1, 2)[i]
        at = pl.ds(d * H, H) if i == 0 else pl.ds(0, T)
        return remote(
            b_send.at[u, d, i, at], b_recv.at[u, d, i, at], b_ss.at[u, d, i], b_rs.at[u, d, i],
            on_tp(step if d == 0 else -step),
        )

    def x_copy(src, dst, i, to):
        return remote(x_t.at[src], x_t.at[dst], x_ss.at[dst, i], x_rs.at[dst, i], on_grp(peer(to)))

    def x_half(src, dst, i, to):
        at = pl.ds(i * (D // 2), D // 2)
        return remote(
            x_t.at[src, at], x_t.at[dst, at], x_ss.at[dst, i], x_rs.at[dst, i], on_grp(peer(to))
        )

    def sum_first(u):
        far = part((tp + 4) % nt, u).astype(BF)
        for d in range(2):
            b_send[u, d, 0, d * H : (d + 1) * H] = far[d * H : (d + 1) * H]
            b_send[u, d, 1] = part((tp + (3 if d == 0 else nt - 3)) % nt, u).astype(BF)

    def sum_send(u):
        for i in range(2):
            for d in range(2):
                go(b_copy(u, d, i))

    def sum_near(u):
        for d in range(2):
            b_send[u, d, 2] = part((tp + (1 if d == 0 else nt - 1)) % nt, u).astype(BF)
            go(b_copy(u, d, 2))
        for d in range(2):
            raw[u, d] = part((tp + (2 if d == 0 else nt - 2)) % nt, u)
        mine[u] = part(tp, u)

    def sum_second(u):
        for d in range(2):
            at = slice(d * H, (d + 1) * H)
            b_copy(u, d, 0).wait_recv()
            raw[u, d, at] = raw[u, d, at] + b_recv[u, d, 0, at].astype(F32)
            b_copy(u, d, 1).wait_recv()
            b_send[u, d, 3] = (raw[u, d] + b_recv[u, d, 1].astype(F32)).astype(BF)
            go(b_copy(u, d, 3))

    def sum_end(u):
        total = mine[u]
        for i in (2, 3):
            for d in range(2):
                b_copy(u, d, i).wait_recv()
                total = total + b_recv[u, d, i].astype(F32)
        mine[u] = total

    def c_copy(u, k):
        return remote(kv[u].at[0], kv[u].at[k], c_ss.at[u, k], c_rs.at[u, k], on_grp(peer(k)))

    sum_first(0)
    x_t[0] = x_ref[...].astype(F32).T.astype(BF)
    pl.semaphore_wait(barrier, NG - 1 + nt - 1)
    sum_send(0)
    sum_near(0)
    for k in (1, 2, 4):
        go(x_copy(0, k, 0, k))

    def prep_tables():
        c, s = turned_tables(base_ref, start_ref, NG)
        cos_r[...] = c
        sin_r[...] = s
        o_t[...] = jnp.zeros_like(o_t)

    def prep(c):
        def run():
            at = slice(c * HD, (c + 1) * HD)
            ct = slice(c * T, (c + 1) * T)
            live = lax.broadcasted_iota(jnp.int32, (T, HD), 0) < len_ref[0]
            qf = rotate(q_ref[:, at].astype(F32), cos_r[...], sin_r[...])
            q_rows[c] = qf.astype(BF)
            q_cols[:, ct] = qf.T.astype(BF)
            gf = jnp.where(live, do_ref[:, at].astype(F32), 0.0)
            g_rows[c] = gf.astype(BF)
            g_cols[:, ct] = gf.T.astype(BF)

        return run

    def prep_own():
        kb[own] = rotate(kv_ref[:, :HD].astype(F32), cos_r[...], sin_r[...]).astype(BF)
        vb[own] = kv_ref[:, HD:]

    def scores(p, is_own):
        kt[p] = kb[p].astype(F32).T.astype(BF)
        k = kb[p]
        if is_own:
            visible = lax.broadcasted_iota(jnp.int32, (T, T), 0) <= lax.broadcasted_iota(
                jnp.int32, (T, T), 1
            )
        for c in range(GQ):
            ct = slice(c * T, (c + 1) * T)
            s = dot(k, q_cols[:, ct]) * SCALE
            if is_own:
                s = jnp.where(visible, s, -jnp.inf)
            m = jnp.max(s, axis=0, keepdims=True)
            raised = jnp.exp(s - m)
            e[p, :, ct] = raised
            top[p, :, ct] = m
            low[p, :, ct] = jnp.sum(raised, axis=0, keepdims=True)

    fillers = [prep_tables] + [prep(c) for c in range(GQ)] + [prep_own]

    def fill(count):
        for _ in range(count):
            if fillers:
                fillers.pop(0)()

    fill(4)
    sum_second(0)
    sum_first(1)
    sum_send(1)
    sum_near(1)
    fill(len(fillers))
    scores(own, True)
    sum_end(0)
    cos_p, sin_p = turned_tables(base_ref, start_ref, grp)
    kb[0] = rotate(mine[0], cos_p, sin_p).astype(BF)
    for k in range(1, NG):
        go(c_copy(0, k))
    sum_second(1)
    scores(0, False)
    for k in (1, 2):
        x_copy(0, k, 0, k).wait_recv()
    go(x_half(1, 3, 0, 1))
    go(x_half(2, 3, 1, 2))

    def score_step(k, carry):
        c_copy(0, k).wait_recv()
        scores(k, False)
        return carry

    lax.fori_loop(1, 3, score_step, 0)
    sum_end(1)
    vb[0] = mine[1].astype(BF)
    for k in range(1, NG):
        go(c_copy(1, k))
    lax.fori_loop(3, NG, score_step, 0)
    x_copy(0, 4, 0, 4).wait_recv()
    go(x_copy(4, 5, 0, 1))
    go(x_copy(4, 6, 0, 2))

    m = functools.reduce(jnp.maximum, [top[p] for p in range(NG + 1)])
    weights = [jnp.exp(top[p] - m) for p in range(NG + 1)]
    total = functools.reduce(jnp.add, [weights[p] * low[p] for p in range(NG + 1)])
    inverse = 1.0 / total
    for p in range(NG + 1):
        top[p] = weights[p] * inverse

    def e_copy(u, k):
        return remote(
            grad_send.at[u, k], grad_recv.at[u, k], e_ss.at[u, k], e_rs.at[u, k], on_grp(source(k))
        )

    def weigh(p):
        vt[p] = vb[p].astype(F32).T.astype(BF)
        dv = jnp.zeros((T, HD), F32)
        for c in range(GQ):
            ct = slice(c * T, (c + 1) * T)
            ab = (e[p, :, ct] * top[p, :, ct]).astype(BF)
            o_t[:, ct] += dot(vt[p], ab)
            dv = dv + dot(ab, g_rows[c])
        return dv

    def weigh_step(k, carry):
        c_copy(1, k).wait_recv()
        grad_send[1, k] = weigh(k).astype(BF)
        e_copy(1, k).start()
        return carry

    dkv_ref[:, HD:] = weigh(own).astype(BF)
    lax.fori_loop(1, NG, weigh_step, 0)
    mine[1] = weigh(0)
    for c in range(GQ):
        ct = slice(c * T, (c + 1) * T)
        delta[:, ct] = jnp.sum(
            o_t[:, ct].astype(BF).astype(F32) * g_cols[:, ct].astype(F32), axis=0, keepdims=True
        )

    def backward(p):
        v = vb[p]
        dk = jnp.zeros((T, HD), F32)
        for c in range(GQ):
            ct = slice(c * T, (c + 1) * T)
            a = e[p, :, ct] * top[p, :, ct]
            da = dot(v, g_cols[:, ct])
            ds = (a * (da - delta[:, ct])).astype(BF)
            ds_all[p, :, ct] = ds
            dk = dk + dot(ds, q_rows[c])
        return dk * SCALE

    def grad_step(i, carry):
        k = NG - 1 - i
        grad_send[0, k] = backward(k).astype(BF)
        e_copy(0, k).start()
        return carry

    def gather_sum(u):
        def step(i, carry):
            k = 1 + i if u == 1 else NG - 1 - i
            e_copy(u, k).wait_recv()
            mine[u] = mine[u] + grad_recv[u, k].astype(F32)
            return carry

        lax.fori_loop(0, NG - 1, step, 0)

    def v_copy(step):
        return remote(
            heads.at[1, 0], heads.at[1, nt - step], f_ss.at[1, step], f_rs.at[1, step], on_tp(step)
        )

    def k_copy(d, i):
        at = pl.ds(d * H, H) if i == 3 else pl.ds(0, T)
        step = (1, 2, 1, 2)[i]
        src = (0, 0, 2, 2)[i]
        dst = (1, 2, 3, 4)[i]
        if d == 0:
            src, dst = (nt - src) % nt, nt - dst
        return remote(
            heads.at[0, src, at], heads.at[0, dst, at], f_ss.at[0, d * 4 + i], f_rs.at[0, d * 4 + i],
            on_tp(step if d == 0 else -step),
        )

    def a_copy(u, slot):
        return remote(
            heads.at[u, slot], cols.at[u, grp], a_ss.at[u, slot], a_rs.at[u, grp], on_grp((tp + slot) % nt)
        )

    def pass_on(u, slot):
        @pl.when((tp + slot) % nt != grp)
        def _():
            a_copy(u, slot).start()

    def hidden(u, slot, first=False):
        h = (tp + slot) % nt
        at = pl.ds(pl.multiple_of(h * W2 + u * HD, HD), HD)
        term = lax.dot_general(
            heads[u, slot], w_ref[:, at], (((1,), (1,)), ((), ())), preferred_element_type=F32
        )
        if first:
            dh_acc[...] = term
        else:
            dh_acc[...] += term

    def query_out(c):
        ct = slice(c * T, (c + 1) * T)
        dq = jnp.zeros((HD, T), F32)
        for p in range(NG + 1):
            dq = dq + dot(kt[p], ds_all[p, :, ct])
        dq_ref[:, c * HD : (c + 1) * HD] = rotate(dq.T * SCALE, cos_r[...], -sin_r[...]).astype(BF)

    lax.fori_loop(0, 2, grad_step, 0)
    gather_sum(1)
    heads[1, 0] = mine[1].astype(BF)
    for step in (1, nt - 1, 2, nt - 2, 3, nt - 3, 4):
        go(v_copy(step))
    pass_on(1, 0)
    lax.fori_loop(2, 5, grad_step, 0)
    for k in (5, 6):
        x_copy(4, k, 0, 1).wait_recv()
    go(x_half(5, 7, 0, 1))
    go(x_half(6, 7, 1, 2))
    lax.fori_loop(5, NG - 1, grad_step, 0)
    mine[0] = backward(0)
    gather_sum(0)
    cos_p, sin_p = turned_tables(base_ref, start_ref, grp)
    heads[0, 0] = rotate(mine[0], cos_p, -sin_p).astype(BF)
    for i in (1, 0):
        for d in range(2):
            go(k_copy(d, i))
    pass_on(0, 0)
    for step in (1, nt - 1, 2, nt - 2, 3, nt - 3, 4):
        v_copy(step).wait_recv()
        pass_on(1, nt - step)
    dk = backward(own)
    dkv_ref[:, :HD] = rotate(dk, cos_r[...], -sin_r[...]).astype(BF)
    for d in range(2):
        k_copy(d, 1).wait_recv()
        for i in (2, 3):
            go(k_copy(d, i))
    for i in (1, 0):
        for d in range(2):
            if i == 0:
                k_copy(d, i).wait_recv()
            pass_on(0, nt - i - 1 if d == 0 else i + 1)
    for c in range(4):
        query_out(c)
    for d in range(2):
        k_copy(d, 2).wait_recv()
        pass_on(0, nt - 3 if d == 0 else 3)
    for d in range(2):
        k_copy(d, 3).wait_recv()
    pass_on(0, 4)
    for c in range(4, GQ):
        query_out(c)
    hidden(1, 0, True)
    for slot in range(1, nt):
        hidden(1, slot)
    for slot in range(nt):
        hidden(0, slot)

    def x_end():
        for i in range(2):
            x_half(1, 3, i, 1).wait_recv()
            x_half(1, 7, i, 1).wait_recv()

    def weight_step(u):
        def step(k, carry):
            other = source(k)
            remote(
                heads.at[u, 0], cols.at[u, other], a_ss.at[u, 0], a_rs.at[u, other], on_grp(peer(1))
            ).wait_recv()
            dw_ref[:, u * HD : (u + 1) * HD] += dot(x_t[k], cols[u, other])
            return carry

        return step

    dh_ref[...] = dh_acc[...].astype(BF)
    x_end()
    dw_ref[:, HD:] = dot(x_t[0], heads[1, (grp - tp + nt) % nt])
    lax.fori_loop(1, NG, weight_step(1), 0)
    dw_ref[:, :HD] = dot(x_t[0], heads[0, (grp - tp + nt) % nt])
    lax.fori_loop(1, NG, weight_step(0), 0)

    for copy in started:
        copy.wait_send()

    def end_step(k, carry):
        e_copy(0, k).wait_send()
        e_copy(1, k).wait_send()
        return carry

    lax.fori_loop(1, NG, end_step, 0)
    for slot in range(nt):

        @pl.when((tp + slot) % nt != grp)
        def _():
            a_copy(0, slot).wait_send()
            a_copy(1, slot).wait_send()


def hand_over(*refs):
    n = len(refs) // 2
    for i in range(n):
        refs[n + i][...] = refs[i][...]


def local(nx, nt, prompt_hidden, w_kv, resp_q, resp_kv, d_out, lengths):
    T, D = prompt_hidden.shape
    NG = 2 * nx
    W2 = 2 * HD
    base, start = tables(T, NG + 1)
    start = start[:, None]
    vm = pl.BlockSpec(memory_space=pltpu.VMEM)
    dma = pltpu.SemaphoreType.DMA
    results = pl.pallas_call(
        functools.partial(kernel, nx, nt),
        out_shape=(
            jax.ShapeDtypeStruct((T, GQ * HD), BF),
            jax.ShapeDtypeStruct((T, W2), BF),
            jax.ShapeDtypeStruct((T, D), BF),
            jax.ShapeDtypeStruct((D, W2), F32),
        ),
        in_specs=[vm] * 5 + [pl.BlockSpec(memory_space=pltpu.SMEM)] + [vm] * 2,
        out_specs=(vm,) * 4,
        scratch_shapes=[
            pltpu.VMEM((GQ, T, HD), BF),
            pltpu.VMEM((HD, GQ * T), BF),
            pltpu.VMEM((GQ, T, HD), BF),
            pltpu.VMEM((HD, GQ * T), BF),
            pltpu.VMEM((NG + 1, T, HD), BF),
            pltpu.VMEM((NG + 1, T, HD), BF),
            pltpu.VMEM((NG + 1, HD, T), BF),
            pltpu.VMEM((NG + 1, HD, T), BF),
            pltpu.VMEM((NG + 1, T, GQ * T), F32),
            pltpu.VMEM((NG + 1, 1, GQ * T), F32),
            pltpu.VMEM((NG + 1, 1, GQ * T), F32),
            pltpu.VMEM((1, GQ * T), F32),
            pltpu.VMEM((NG + 1, T, GQ * T), BF),
            pltpu.VMEM((HD, GQ * T), F32),
            pltpu.VMEM((T, HD), F32),
            pltpu.VMEM((T, HD), F32),
            pltpu.VMEM((2, 2, 4, T, HD), BF),
            pltpu.VMEM((2, 2, 4, T, HD), BF),
            pltpu.VMEM((2, 2, T, HD), F32),
            pltpu.VMEM((2, T, HD), F32),
            pltpu.VMEM((NG, D, T), BF),
            pltpu.VMEM((2, NG, T, HD), BF),
            pltpu.VMEM((2, NG, T, HD), BF),
            pltpu.VMEM((2, nt, T, HD), BF),
            pltpu.VMEM((2, NG, T, HD), BF),
            pltpu.VMEM((T, D), F32),
            dma((2, 2, 4)),
            dma((2, 2, 4)),
            dma((NG, 2)),
            dma((NG, 2)),
            dma((2, NG)),
            dma((2, NG)),
            dma((2, NG)),
            dma((2, NG)),
            dma((2, nt)),
            dma((2, nt)),
            dma((2, nt)),
            dma((2, NG)),
        ],
        compiler_params=pltpu.CompilerParams(
            collective_id=0, has_side_effects=True, vmem_limit_bytes=60 * 2**20
        ),
        name="prefix_attention_backward",
    )(
        prompt_hidden,
        w_kv,
        resp_q.reshape(T, GQ * HD),
        d_out.reshape(T, GQ * HD),
        resp_kv.reshape(T, W2),
        lengths,
        jnp.asarray(base),
        jnp.asarray(start),
    )
    dq, dkv, dh, dw = pl.pallas_call(
        hand_over,
        out_shape=tuple(jax.ShapeDtypeStruct(r.shape, r.dtype) for r in results),
        in_specs=[vm] * 4,
        out_specs=(vm,) * 4,
        name="hand_over",
    )(*results)
    return dq[None], dkv[None], dh, dw


def solution(mesh):
    nx = mesh.shape["grp"] // 2
    nt = mesh.shape["tp"]
    return jax.shard_map(
        functools.partial(local, nx, nt),
        mesh=mesh,
        in_specs=(
            P(("dp", "grp"), "tp"),
            P("tp", None),
            P(("dp", "grp"), None, "tp"),
            P(("dp", "grp"), None, "tp"),
            P(("dp", "grp"), None, "tp"),
            P(("dp", "grp")),
        ),
        out_specs=(
            P(("dp", "grp"), None, "tp"),
            P(("dp", "grp"), None, "tp"),
            P(("dp", "grp"), "tp"),
            P(("dp", "tp"), "grp"),
        ),
        check_vma=False,
    )
```

time: 105 us -> 87.3 us (0.83)
  Pallas kernels: 95.6 us -> 85.8 us
  local copies, waits for them, and re-layouts: 7.12 us -> 0 us
    pallas_call x1, Pallas kernels: 95.6 us -> 83.3 us  [local(): pl.pallas_call(functools.partial(kernel, nx, nt), out_shape=(jax.ShapeDty...]
    unnamed x4 -> x0, local copies, waits for them, and re-layouts: 7.12 us -> none
    pallas_call x0 -> x1, Pallas kernels: none -> 2.59 us  [local(): pl.pallas_call(hand_over, out_shape=tuple((jax.ShapeDtypeStruct(r.shape,...]
where the time goes in v2:
time: 87.3 us; the launch traced here: 87.1 us
  Pallas kernels  85.8 us (98%)
  between operations  1.29 us (1%)
    pallas_call x1, Pallas kernels, local(): pl.pallas_call(functools.partial(kernel, nx, nt), out_shape=(jax.ShapeDty...  83.3 us
    pallas_call x1, Pallas kernels, local(): pl.pallas_call(hand_over, out_shape=tuple((jax.ShapeDtypeStruct(r.shape,...  2.59 us

profile of v2, /device:TPU:4, one launch (start us, length us, event | category | flops | bytes accessed | tf_op | source)
XLA Modules:
  0.0 87.1 jit_solution(12146887951277664880)
XLA Ops:
  1.3 83.3 %prefix_attention_backward.1 = (bf16[256,1024]{1,0:T(8,128)(2,1)}, bf16[256,256]{1,0:T(8,128)(2,1)}, bf16[256,640]{1,0:T(8,128)(2,1)}, f32[640,256]{1,0:T(8,128)}) custom-call(bf16[256,640]{1,0:T(8,128)(2,1)} %x_ref.1, bf16[640,2048]{1,0:T(8,128)(2,1)} %w_ref.1, bf16[256,1024]{1,0:T(8,128)(2,1)} %bitcast.5, bf16[256,1024]{1,0:T(8,128)(2,1)} %bitcast.6, ...), custom_call_target="tpu_custom_call" | custom-call | tf_op jit(solution)/shard_map/prefix_attention_backward/pallas_call | solution.py:463
  84.5 2.6 %hand_over.1 = (bf16[256,1024]{1,0:T(8,128)(2,1)}, bf16[256,256]{1,0:T(8,128)(2,1)}, bf16[256,640]{1,0:T(8,128)(2,1)}, f32[640,256]{1,0:T(8,128)}) custom-call(bf16[256,1024]{1,0:T(8,128)(2,1)} %get-tuple-element.12.refs_0_, bf16[256,256]{1,0:T(8,128)(2,1)} %get-tuple-element.13.refs_1_, bf16[256,640]{1,0:T(8,128)(2,1)} %get-tuple-element.14.refs_2_, ...), custom_call_target="tpu_custom_call" | custom-call | tf_op jit(solution)/shard_map/hand_over/pallas_call | solution.py:527

commit v3 on v2

--- a/solution.py
+++ b/solution.py
@@ -12,6 +12,7 @@
 GQ = 8
 THETA = 1000000.0
 SCALE = HD**-0.5
+SCALE2 = SCALE * float(np.log2(np.e))
 MESH = pl.DeviceIdType.MESH
 BF = jnp.bfloat16
 F32 = jnp.float32
@@ -45,11 +46,12 @@
 
 
 def kernel(
-    nx, nt, x_ref, w_ref, q_ref, do_ref, kv_ref, len_ref, base_ref, start_ref,
-    dq_ref, dkv_ref, dh_ref, dw_ref,
-    q_rows, q_cols, g_rows, g_cols, kb, vb, kt, vt, e, top, low, delta, ds_all, o_t, cos_r, sin_r,
+    nx, nt, x_in, w_in, q_in, do_in, kv_in, len_ref, base_in, start_ref,
+    dq_out, dkv_out, dh_out, dw_out,
+    x_ref, w_ref, q_ref, do_ref, kv_ref, base_ref, dq_ref, dkv_ref, dh_ref, dw_ref,
+    q_rows, q_cols, g_rows, g_cols, kb, vb, kt, vt, e, top, low, delta, ds_all, cos_r, sin_r,
     b_send, b_recv, raw, mine, x_t, grad_send, grad_recv, heads, cols, dh_acc,
-    b_ss, b_rs, x_ss, x_rs, c_ss, c_rs, e_ss, e_rs, f_ss, f_rs, a_ss, a_rs,
+    b_ss, b_rs, x_ss, x_rs, c_ss, c_rs, e_ss, e_rs, f_ss, f_rs, a_ss, a_rs, in_sems, out_sems,
 ):
     T = x_ref.shape[0]
     D = x_ref.shape[1]
@@ -96,6 +98,15 @@
     for step in range(1, nt):
         pl.semaphore_signal(barrier, inc=1, device_id=on_tp(step), device_id_type=MESH)
 
+    loads = [
+        pltpu.make_async_copy(src, dst, in_sems.at[i])
+        for i, (src, dst) in enumerate(
+            [(x_in, x_ref), (w_in, w_ref), (base_in, base_ref), (q_in, q_ref), (do_in, do_ref), (kv_in, kv_ref)]
+        )
+    ]
+    for load in loads:
+        load.start()
+
     def part(h, u):
         at = pl.ds(pl.multiple_of(h * W2 + u * HD, HD), HD)
         return dot(x_ref[...], w_ref[:, at])
@@ -156,8 +167,10 @@
     def c_copy(u, k):
         return remote(kv[u].at[0], kv[u].at[k], c_ss.at[u, k], c_rs.at[u, k], on_grp(peer(k)))
 
+    loads[0].wait()
+    x_t[0] = x_ref[...].astype(F32).T.astype(BF)
+    loads[1].wait()
     sum_first(0)
-    x_t[0] = x_ref[...].astype(F32).T.astype(BF)
     pl.semaphore_wait(barrier, NG - 1 + nt - 1)
     sum_send(0)
     sum_near(0)
@@ -168,7 +181,6 @@
         c, s = turned_tables(base_ref, start_ref, NG)
         cos_r[...] = c
         sin_r[...] = s
-        o_t[...] = jnp.zeros_like(o_t)
 
     def prep(c):
         def run():
@@ -197,11 +209,11 @@
             )
         for c in range(GQ):
             ct = slice(c * T, (c + 1) * T)
-            s = dot(k, q_cols[:, ct]) * SCALE
+            s = dot(k, q_cols[:, ct])
             if is_own:
                 s = jnp.where(visible, s, -jnp.inf)
-            m = jnp.max(s, axis=0, keepdims=True)
-            raised = jnp.exp(s - m)
+            m = jnp.max(s, axis=0, keepdims=True) * SCALE2
+            raised = jnp.exp2(s * SCALE2 - m)
             e[p, :, ct] = raised
             top[p, :, ct] = m
             low[p, :, ct] = jnp.sum(raised, axis=0, keepdims=True)
@@ -213,6 +225,8 @@
             if fillers:
                 fillers.pop(0)()
 
+    for load in loads[2:]:
+        load.wait()
     fill(4)
     sum_second(0)
     sum_first(1)
@@ -220,6 +234,10 @@
     sum_near(1)
     fill(len(fillers))
     scores(own, True)
+    for k in (1, 2):
+        x_copy(0, k, 0, k).wait_recv()
+    go(x_half(1, 3, 0, 1))
+    go(x_half(2, 3, 1, 2))
     sum_end(0)
     cos_p, sin_p = turned_tables(base_ref, start_ref, grp)
     kb[0] = rotate(mine[0], cos_p, sin_p).astype(BF)
@@ -227,28 +245,22 @@
         go(c_copy(0, k))
     sum_second(1)
     scores(0, False)
-    for k in (1, 2):
-        x_copy(0, k, 0, k).wait_recv()
-    go(x_half(1, 3, 0, 1))
-    go(x_half(2, 3, 1, 2))
 
     def score_step(k, carry):
         c_copy(0, k).wait_recv()
         scores(k, False)
         return carry
 
-    lax.fori_loop(1, 3, score_step, 0)
+    for k in range(1, 3):
+        score_step(k, 0)
     sum_end(1)
     vb[0] = mine[1].astype(BF)
     for k in range(1, NG):
         go(c_copy(1, k))
-    lax.fori_loop(3, NG, score_step, 0)
-    x_copy(0, 4, 0, 4).wait_recv()
-    go(x_copy(4, 5, 0, 1))
-    go(x_copy(4, 6, 0, 2))
-
+    for k in range(3, NG):
+        score_step(k, 0)
     m = functools.reduce(jnp.maximum, [top[p] for p in range(NG + 1)])
-    weights = [jnp.exp(top[p] - m) for p in range(NG + 1)]
+    weights = [jnp.exp2(top[p] - m) for p in range(NG + 1)]
     total = functools.reduce(jnp.add, [weights[p] * low[p] for p in range(NG + 1)])
     inverse = 1.0 / total
     for p in range(NG + 1):
@@ -265,7 +277,7 @@
         for c in range(GQ):
             ct = slice(c * T, (c + 1) * T)
             ab = (e[p, :, ct] * top[p, :, ct]).astype(BF)
-            o_t[:, ct] += dot(vt[p], ab)
+            ds_all[p, :, ct] = ab
             dv = dv + dot(ab, g_rows[c])
         return dv
 
@@ -276,25 +288,26 @@
         return carry
 
     dkv_ref[:, HD:] = weigh(own).astype(BF)
-    lax.fori_loop(1, NG, weigh_step, 0)
+    for k in range(1, NG):
+        weigh_step(k, 0)
     mine[1] = weigh(0)
     for c in range(GQ):
         ct = slice(c * T, (c + 1) * T)
+        out = jnp.zeros((HD, T), F32)
+        for p in range(NG + 1):
+            out = out + dot(vt[p], ds_all[p, :, ct])
         delta[:, ct] = jnp.sum(
-            o_t[:, ct].astype(BF).astype(F32) * g_cols[:, ct].astype(F32), axis=0, keepdims=True
+            out.astype(BF).astype(F32) * g_cols[:, ct].astype(F32), axis=0, keepdims=True
         )
 
     def backward(p):
         v = vb[p]
-        dk = jnp.zeros((T, HD), F32)
         for c in range(GQ):
             ct = slice(c * T, (c + 1) * T)
             a = e[p, :, ct] * top[p, :, ct]
             da = dot(v, g_cols[:, ct])
-            ds = (a * (da - delta[:, ct])).astype(BF)
-            ds_all[p, :, ct] = ds
-            dk = dk + dot(ds, q_rows[c])
-        return dk * SCALE
+            ds_all[p, :, ct] = (a * (da - delta[:, ct])).astype(BF)
+        return dot(ds_all[p], q_rows[...].reshape(GQ * T, HD)) * SCALE
 
     def grad_step(i, carry):
         k = NG - 1 - i
@@ -311,12 +324,7 @@
 
         lax.fori_loop(0, NG - 1, step, 0)
 
-    def v_copy(step):
-        return remote(
-            heads.at[1, 0], heads.at[1, nt - step], f_ss.at[1, step], f_rs.at[1, step], on_tp(step)
-        )
-
-    def k_copy(d, i):
+    def f_copy(u, d, i):
         at = pl.ds(d * H, H) if i == 3 else pl.ds(0, T)
         step = (1, 2, 1, 2)[i]
         src = (0, 0, 2, 2)[i]
@@ -324,9 +332,34 @@
         if d == 0:
             src, dst = (nt - src) % nt, nt - dst
         return remote(
-            heads.at[0, src, at], heads.at[0, dst, at], f_ss.at[0, d * 4 + i], f_rs.at[0, d * 4 + i],
+            heads.at[u, src, at], heads.at[u, dst, at], f_ss.at[u, d * 4 + i], f_rs.at[u, d * 4 + i],
             on_tp(step if d == 0 else -step),
         )
+
+    def f_first(u):
+        for i in (1, 0):
+            for d in range(2):
+                go(f_copy(u, d, i))
+        pass_on(u, 0)
+
+    def f_second(u):
+        for d in range(2):
+            f_copy(u, d, 1).wait_recv()
+            for i in (3, 2):
+                go(f_copy(u, d, i))
+        for d in range(2):
+            pass_on(u, nt - 2 if d == 0 else 2)
+        for d in range(2):
+            f_copy(u, d, 0).wait_recv()
+            pass_on(u, nt - 1 if d == 0 else 1)
+
+    def f_third(u):
+        for d in range(2):
+            f_copy(u, d, 2).wait_recv()
+            pass_on(u, nt - 3 if d == 0 else 3)
+        for d in range(2):
+            f_copy(u, d, 3).wait_recv()
+        pass_on(u, 4)
 
     def a_copy(u, slot):
         return remote(
@@ -356,78 +389,79 @@
             dq = dq + dot(kt[p], ds_all[p, :, ct])
         dq_ref[:, c * HD : (c + 1) * HD] = rotate(dq.T * SCALE, cos_r[...], -sin_r[...]).astype(BF)
 
-    lax.fori_loop(0, 2, grad_step, 0)
+    for i in range(3):
+        grad_step(i, 0)
     gather_sum(1)
     heads[1, 0] = mine[1].astype(BF)
-    for step in (1, nt - 1, 2, nt - 2, 3, nt - 3, 4):
-        go(v_copy(step))
-    pass_on(1, 0)
-    lax.fori_loop(2, 5, grad_step, 0)
-    for k in (5, 6):
-        x_copy(4, k, 0, 1).wait_recv()
-    go(x_half(5, 7, 0, 1))
-    go(x_half(6, 7, 1, 2))
-    lax.fori_loop(5, NG - 1, grad_step, 0)
+    f_first(1)
+    for i in range(3, NG - 1):
+        grad_step(i, 0)
     mine[0] = backward(0)
+    f_second(1)
+    x_copy(0, 4, 0, 4).wait_recv()
+    go(x_copy(4, 5, 0, 1))
+    go(x_copy(4, 6, 0, 2))
+    for i in range(2):
+        x_half(1, 3, i, 1).wait_recv()
+    go(x_copy(3, 7, 0, 4))
     gather_sum(0)
     cos_p, sin_p = turned_tables(base_ref, start_ref, grp)
     heads[0, 0] = rotate(mine[0], cos_p, -sin_p).astype(BF)
-    for i in (1, 0):
-        for d in range(2):
-            go(k_copy(d, i))
-    pass_on(0, 0)
-    for step in (1, nt - 1, 2, nt - 2, 3, nt - 3, 4):
-        v_copy(step).wait_recv()
-        pass_on(1, nt - step)
+    f_first(0)
+    f_third(1)
     dk = backward(own)
     dkv_ref[:, :HD] = rotate(dk, cos_r[...], -sin_r[...]).astype(BF)
-    for d in range(2):
-        k_copy(d, 1).wait_recv()
-        for i in (2, 3):
-            go(k_copy(d, i))
-    for i in (1, 0):
-        for d in range(2):
-            if i == 0:
-                k_copy(d, i).wait_recv()
-            pass_on(0, nt - i - 1 if d == 0 else i + 1)
+    stores = [
+        pltpu.make_async_copy(src, dst, out_sems.at[i])
+        for i, (src, dst) in enumerate(
+            [
+                (dkv_ref, dkv_out),
+                (dq_ref, dq_out),
+                (dh_ref, dh_out),
+                (dw_ref.at[:, pl.ds(HD, HD)], dw_out.at[:, pl.ds(HD, HD)]),
+                (dw_ref.at[:, pl.ds(0, HD)], dw_out.at[:, pl.ds(0, HD)]),
+            ]
+        )
+    ]
+    stores[0].start()
+    f_second(0)
     for c in range(4):
         query_out(c)
-    for d in range(2):
-        k_copy(d, 2).wait_recv()
-        pass_on(0, nt - 3 if d == 0 else 3)
-    for d in range(2):
-        k_copy(d, 3).wait_recv()
-    pass_on(0, 4)
+    f_third(0)
     for c in range(4, GQ):
         query_out(c)
+    stores[1].start()
     hidden(1, 0, True)
     for slot in range(1, nt):
         hidden(1, slot)
     for slot in range(nt):
         hidden(0, slot)
 
-    def x_end():
-        for i in range(2):
-            x_half(1, 3, i, 1).wait_recv()
-            x_half(1, 7, i, 1).wait_recv()
-
-    def weight_step(u):
-        def step(k, carry):
+    def weights_out(u):
+        def arrived(k, carry):
             other = source(k)
             remote(
                 heads.at[u, 0], cols.at[u, other], a_ss.at[u, 0], a_rs.at[u, other], on_grp(peer(1))
             ).wait_recv()
-            dw_ref[:, u * HD : (u + 1) * HD] += dot(x_t[k], cols[u, other])
             return carry
 
-        return step
+        lax.fori_loop(1, NG, arrived, 0)
+        cols[u, grp] = heads[u, (grp - tp + nt) % nt]
+        for i in range(2):
+            at = slice(i * D // 2, (i + 1) * D // 2)
+            total = dot(x_t[0, at], cols[u, grp])
+            for k in range(1, NG):
+                total = total + dot(x_t[k, at], cols[u, source(k)])
+            dw_ref[at, u * HD : (u + 1) * HD] = total
 
     dh_ref[...] = dh_acc[...].astype(BF)
-    x_end()
-    dw_ref[:, HD:] = dot(x_t[0], heads[1, (grp - tp + nt) % nt])
-    lax.fori_loop(1, NG, weight_step(1), 0)
-    dw_ref[:, :HD] = dot(x_t[0], heads[0, (grp - tp + nt) % nt])
-    lax.fori_loop(1, NG, weight_step(0), 0)
+    stores[2].start()
+    for k in (5, 6, 7):
+        x_copy(4, k, 0, 1).wait_recv()
+    weights_out(1)
+    stores[3].start()
+    weights_out(0)
+    stores[4].start()
 
     for copy in started:
         copy.wait_send()
@@ -444,6 +478,9 @@
         def _():
             a_copy(0, slot).wait_send()
             a_copy(1, slot).wait_send()
+
+    for store in stores:
+        store.wait()
 
 
 def hand_over(*refs):
@@ -459,6 +496,7 @@
     base, start = tables(T, NG + 1)
     start = start[:, None]
     vm = pl.BlockSpec(memory_space=pltpu.VMEM)
+    hbm = pl.BlockSpec(memory_space=pl.ANY)
     dma = pltpu.SemaphoreType.DMA
     results = pl.pallas_call(
         functools.partial(kernel, nx, nt),
@@ -468,9 +506,19 @@
             jax.ShapeDtypeStruct((T, D), BF),
             jax.ShapeDtypeStruct((D, W2), F32),
         ),
-        in_specs=[vm] * 5 + [pl.BlockSpec(memory_space=pltpu.SMEM)] + [vm] * 2,
-        out_specs=(vm,) * 4,
+        in_specs=[hbm] * 5 + [pl.BlockSpec(memory_space=pltpu.SMEM)] + [hbm, vm],
+        out_specs=(hbm,) * 4,
         scratch_shapes=[
+            pltpu.VMEM((T, D), BF),
+            pltpu.VMEM((D, nt * W2), BF),
+            pltpu.VMEM((T, GQ * HD), BF),
+            pltpu.VMEM((T, GQ * HD), BF),
+            pltpu.VMEM((T, W2), BF),
+            pltpu.VMEM((T, W2), F32),
+            pltpu.VMEM((T, GQ * HD), BF),
+            pltpu.VMEM((T, W2), BF),
+            pltpu.VMEM((T, D), BF),
+            pltpu.VMEM((D, W2), F32),
             pltpu.VMEM((GQ, T, HD), BF),
             pltpu.VMEM((HD, GQ * T), BF),
             pltpu.VMEM((GQ, T, HD), BF),
@@ -484,7 +532,6 @@
             pltpu.VMEM((NG + 1, 1, GQ * T), F32),
             pltpu.VMEM((1, GQ * T), F32),
             pltpu.VMEM((NG + 1, T, GQ * T), BF),
-            pltpu.VMEM((HD, GQ * T), F32),
             pltpu.VMEM((T, HD), F32),
             pltpu.VMEM((T, HD), F32),
             pltpu.VMEM((2, 2, 4, T, HD), BF),
@@ -509,6 +556,8 @@
             dma((2, nt)),
             dma((2, nt)),
             dma((2, NG)),
+            dma((6,)),
+            dma((5,)),
         ],
         compiler_params=pltpu.CompilerParams(
             collective_id=0, has_side_effects=True, vmem_limit_bytes=60 * 2**20

time: 87.3 us -> 81 us (0.928)
  Pallas kernels: 85.8 us -> 79.6 us
    pallas_call x1, Pallas kernels: 83.3 us -> 77 us  [local(): pl.pallas_call(functools.partial(kernel, nx, nt), out_shape=(jax.ShapeDty...]
where the time goes in v3:
time: 81 us; the launch traced here: 80.8 us
  Pallas kernels  79.6 us (98%)
  between operations  1.29 us (2%)
    pallas_call x1, Pallas kernels, local(): pl.pallas_call(functools.partial(kernel, nx, nt), out_shape=(jax.ShapeDty...  77 us
    pallas_call x1, Pallas kernels, local(): pl.pallas_call(hand_over, out_shape=tuple((jax.ShapeDtypeStruct(r.shape,...  2.59 us

profile of v3, /device:TPU:4, one launch (start us, length us, event | category | flops | bytes accessed | tf_op | source)
XLA Modules:
  0.0 80.8 jit_solution(4654040355748713357)
XLA Ops:
  1.3 77.0 %prefix_attention_backward.1 = (bf16[256,1024]{1,0:T(8,128)(2,1)}, bf16[256,256]{1,0:T(8,128)(2,1)}, bf16[256,640]{1,0:T(8,128)(2,1)}, f32[640,256]{1,0:T(8,128)}) custom-call(bf16[256,640]{1,0:T(8,128)(2,1)} %x_in.1, bf16[640,2048]{1,0:T(8,128)(2,1)} %w_in.1, bf16[256,1024]{1,0:T(8,128)(2,1)} %bitcast.5, bf16[256,1024]{1,0:T(8,128)(2,1)} %bitcast.6, ...), custom_call_target="tpu_custom_call" | custom-call | tf_op jit(solution)/shard_map/prefix_attention_backward/pallas_call | solution.py:501
  78.3 2.6 %hand_over.1 = (bf16[256,1024]{1,0:T(8,128)(2,1)}, bf16[256,256]{1,0:T(8,128)(2,1)}, bf16[256,640]{1,0:T(8,128)(2,1)}, f32[640,256]{1,0:T(8,128)}) custom-call(bf16[256,1024]{1,0:T(8,128)(2,1)} %get-tuple-element.12.refs_0_, bf16[256,256]{1,0:T(8,128)(2,1)} %get-tuple-element.13.refs_1_, bf16[256,640]{1,0:T(8,128)(2,1)} %get-tuple-element.14.refs_2_, ...), custom_call_target="tpu_custom_call" | custom-call | tf_op jit(solution)/shard_map/hand_over/pallas_call | solution.py:576

commit v4 on v3

--- a/solution.py
+++ b/solution.py
@@ -234,10 +234,6 @@
     sum_near(1)
     fill(len(fillers))
     scores(own, True)
-    for k in (1, 2):
-        x_copy(0, k, 0, k).wait_recv()
-    go(x_half(1, 3, 0, 1))
-    go(x_half(2, 3, 1, 2))
     sum_end(0)
     cos_p, sin_p = turned_tables(base_ref, start_ref, grp)
     kb[0] = rotate(mine[0], cos_p, sin_p).astype(BF)
@@ -257,6 +253,10 @@
     vb[0] = mine[1].astype(BF)
     for k in range(1, NG):
         go(c_copy(1, k))
+    for k in (1, 2):
+        x_copy(0, k, 0, k).wait_recv()
+    go(x_half(1, 3, 0, 1))
+    go(x_half(2, 3, 1, 2))
     for k in range(3, NG):
         score_step(k, 0)
     m = functools.reduce(jnp.maximum, [top[p] for p in range(NG + 1)])
@@ -288,9 +288,9 @@
         return carry
 
     dkv_ref[:, HD:] = weigh(own).astype(BF)
+    mine[1] = weigh(0)
     for k in range(1, NG):
         weigh_step(k, 0)
-    mine[1] = weigh(0)
     for c in range(GQ):
         ct = slice(c * T, (c + 1) * T)
         out = jnp.zeros((HD, T), F32)
@@ -389,12 +389,12 @@
             dq = dq + dot(kt[p], ds_all[p, :, ct])
         dq_ref[:, c * HD : (c + 1) * HD] = rotate(dq.T * SCALE, cos_r[...], -sin_r[...]).astype(BF)
 
-    for i in range(3):
+    for i in range(6):
         grad_step(i, 0)
     gather_sum(1)
     heads[1, 0] = mine[1].astype(BF)
     f_first(1)
-    for i in range(3, NG - 1):
+    for i in range(6, NG - 1):
         grad_step(i, 0)
     mine[0] = backward(0)
     f_second(1)

time: 81 us -> 76 us (0.938)
  Pallas kernels: 79.6 us -> 74.6 us
    pallas_call x1, Pallas kernels: 77 us -> 72 us  [local(): pl.pallas_call(functools.partial(kernel, nx, nt), out_shape=(jax.ShapeDty...]
where the time goes in v4:
time: 76 us; the launch traced here: 75.9 us
  Pallas kernels  74.6 us (98%)
  between operations  1.29 us (2%)
    pallas_call x1, Pallas kernels, local(): pl.pallas_call(functools.partial(kernel, nx, nt), out_shape=(jax.ShapeDty...  72 us
    pallas_call x1, Pallas kernels, local(): pl.pallas_call(hand_over, out_shape=tuple((jax.ShapeDtypeStruct(r.shape,...  2.59 us

profile of v4, /device:TPU:4, one launch (start us, length us, event | category | flops | bytes accessed | tf_op | source)
XLA Modules:
  0.0 75.9 jit_solution(16886853696314580221)
XLA Ops:
  1.3 72.0 %prefix_attention_backward.1 = (bf16[256,1024]{1,0:T(8,128)(2,1)}, bf16[256,256]{1,0:T(8,128)(2,1)}, bf16[256,640]{1,0:T(8,128)(2,1)}, f32[640,256]{1,0:T(8,128)}) custom-call(bf16[256,640]{1,0:T(8,128)(2,1)} %x_in.1, bf16[640,2048]{1,0:T(8,128)(2,1)} %w_in.1, bf16[256,1024]{1,0:T(8,128)(2,1)} %bitcast.5, bf16[256,1024]{1,0:T(8,128)(2,1)} %bitcast.6, ...), custom_call_target="tpu_custom_call" | custom-call | tf_op jit(solution)/shard_map/prefix_attention_backward/pallas_call | solution.py:501
  73.3 2.6 %hand_over.1 = (bf16[256,1024]{1,0:T(8,128)(2,1)}, bf16[256,256]{1,0:T(8,128)(2,1)}, bf16[256,640]{1,0:T(8,128)(2,1)}, f32[640,256]{1,0:T(8,128)}) custom-call(bf16[256,1024]{1,0:T(8,128)(2,1)} %get-tuple-element.12.refs_0_, bf16[256,256]{1,0:T(8,128)(2,1)} %get-tuple-element.13.refs_1_, bf16[256,640]{1,0:T(8,128)(2,1)} %get-tuple-element.14.refs_2_, ...), custom_call_target="tpu_custom_call" | custom-call | tf_op jit(solution)/shard_map/hand_over/pallas_call | solution.py:576
